TPU v7x, 32 devices: a whole 2x2x4 slice. The times are simulated.
32 devices in a mesh: dp: 4 (over z), mp: 4 (over y, x), section: 2 (over core).
Axes of the slice: x: 2, y: 2, z: 4, core: 2. Of those that a mesh axis runs over, the one named last changes fastest.
Arguments:
- text_embeds: bfloat16 [3072, 8192], P('dp', 'mp')
- image_rows: bfloat16 [1536, 8192], P('dp', ('mp', 'section'))
- image_source: int32 [3072], P('dp'), may hold values from -1 to 1535, as said below
- live_len: int32 [4], P('dp'), may hold values from 192 to 768, as said below
- norm_gain: bfloat16 [8192], P(('mp', 'section')), may hold values from 0.25 to 1.75
Outputs:
- hessian: float32 [8192, 8192], P('dp', ('mp', 'section'))
Inputs may be any that keep to these rules, and one draw needn't show every extreme that they name: `image_source`: every image row is placed at exactly one token; the tokens of each index of dp hold exactly 384 image rows, and at most 192 of them come from the image rows of any one index of dp, exactly 192 for some pairs in every draw. `live_len`: some index of dp has no padding in every draw.
All inputs are finite; a program needn't handle non-finite values.
Results may differ from a plain program's by a relative error of at most 0.008.
Values may be sent and summed in bfloat16 or wider, within the bound.
A program may use at most 128 MiB of HBM per device.

v0:
```python
import jax
import jax.numpy as jnp
from jax import lax
from jax.sharding import PartitionSpec as P

NORM_EPS = 1e-06


def body(text_embeds, image_rows, image_source, live_len, norm_gain):
    group_count = lax.axis_size("dp")
    feature_groups = lax.axis_size(("mp", "section"))
    tok_rows = text_embeds.shape[0]
    image_count = image_rows.shape[0]
    narrow = image_rows.shape[1]
    capacity = 2 * image_count // group_count
    section_part = lax.axis_index("section")
    own_text = lax.dynamic_slice_in_dim(text_embeds, section_part * narrow, narrow, 1)
    is_image = image_source >= 0
    safe_src = jnp.where(is_image, image_source, 0)
    owner_dev = safe_src // image_count
    local_row = safe_src % image_count
    peer_ids = jnp.arange(group_count, dtype=jnp.int32)
    onehot = ((owner_dev[:, None] == peer_ids[None, :]) & is_image[:, None]).astype(jnp.int32)
    slot_rank = jnp.sum(jnp.cumsum(onehot, axis=0) * onehot, axis=1) - 1
    empty_table = jnp.full((group_count * capacity,), -1, jnp.int32)
    wanted = jnp.where(is_image, owner_dev * capacity + slot_rank, group_count * capacity)
    request_table = empty_table.at[wanted].set(local_row, mode="drop")
    asked_rows = lax.all_to_all(
        request_table.reshape(group_count, capacity), "dp", split_axis=0, concat_axis=0, tiled=True
    )
    is_valid = asked_rows >= 0
    outgoing = image_rows[jnp.where(is_valid, asked_rows, 0)] * is_valid[:, :, None].astype(
        jnp.bfloat16
    )
    incoming = lax.all_to_all(outgoing, "dp", split_axis=0, concat_axis=0, tiled=True)
    wanted_slot = jnp.where(is_image, owner_dev * capacity + slot_rank, 0)
    picked = incoming.reshape(group_count * capacity, narrow)[wanted_slot]
    joined = jnp.where(is_image[:, None], picked, own_text)
    live_mask = (jnp.arange(tok_rows) < live_len[0]).astype(jnp.float32)[:, None]
    widened = joined.astype(jnp.float32)
    squares = lax.psum(jnp.sum(widened * widened, axis=1), ("mp", "section"))
    inverse = lax.rsqrt(squares / (narrow * feature_groups) + NORM_EPS)
    own_cols = (
        widened * inverse[:, None] * norm_gain.astype(jnp.float32)[None, :] * live_mask
    ).astype(jnp.bfloat16)
    contract = (((0,), (0,)), ((), ()))
    all_cols = lax.all_gather(own_cols, ("mp", "section"), axis=1, tiled=True)
    summed = lax.psum_scatter(
        lax.dot_general(all_cols, own_cols, contract, preferred_element_type=jnp.float32).astype(
            jnp.bfloat16
        ),
        "dp",
        scatter_dimension=0,
        tiled=True,
    ).astype(jnp.float32)
    live_count = lax.psum(jnp.sum(live_mask), "dp")
    return summed * (2.0 / live_count)


def solution(mesh):
    in_specs = (P("dp", "mp"), P("dp", ("mp", "section")), P("dp"), P("dp"), P(("mp", "section")))
    out_specs = P("dp", ("mp", "section"))
    return jax.shard_map(body, mesh=mesh, in_specs=in_specs, out_specs=out_specs, check_vma=False)
```

profile of v0, /device:TPU:5, one launch (start us, length us, event | category | flops | bytes accessed | tf_op | source)
XLA Modules:
  0.0 472.7 jit_solution(4002721921620288887)
XLA Ops:
  6.5 0.8 add_select_fusion
  7.3 0.7 add_select_fusion.1
  8.0 1.1 reduce-window.6
  9.2 0.2 slice_reduce_fusion
  9.4 0.2 reduce-window.9
  9.6 0.1 add_bitcast_fusion
  9.7 3.4 scatter_custom_fusion
  13.1 0.1 all_to_all.11
  13.2 8.8 %all_to_all.17 = s32[4,1,192]{2,1,0:T(1,128)S(1)} all-to-all(s32[4,1,192]{2,1,0:T(1,128)S(1)} %all_to_all.11), channel_id=1, replica_groups=mesh['dp'=4,'mp'=4,'section'=2] {'dp'}, dimensions={0} | all-to-all | bytes 6144 | tf_op jit(solution)/shard_map/all_to_all | solution.py:28
  22.0 0.1 reshape.77
  22.1 2.8 gather_fusion
  24.9 1.3 broadcast_multiply_fusion
  26.2 3.6 all-to-all-start.1
  30.6 35.7 %all-to-all-done.1 = bf16[4,192,1024]{2,1,0:T(8,128)(2,1)S(1)} async-done(((bf16[4,192,1024]{2,1,0:T(8,128)(2,1)}), bf16[4,192,1024]{2,1,0:T(8,128)(2,1)S(1)}, u32[]{:S(2)}, u32[]{:S(2)}) %all-to-all-start.1) | async-done | bytes 1572896 | tf_op jit(solution)/shard_map/all_to_all | solution.py:35
  66.2 3.5 gather_fusion.1
  69.8 2.7 fusion
  72.5 12.6 %psum.14 = f32[768]{0:T(1024)S(1)} all-reduce(f32[768]{0:T(1024)S(1)} %fusion), channel_id=1, replica_groups=mesh['dp'=4,'mp'=4,'section'=2] {'mp','section'}, use_global_device_ids=true, to_apply=%region_5.6 | all-reduce | flops 768 | bytes 6144 | tf_op jit(solution)/shard_map/psum | solution.py:41
  85.1 3.0 fusion.3
  88.3 70.3 %all-gather.2.cloned.1.call-done = bf16[768,8192]{1,0:T(8,128)(2,1)} async-done(((bf16[768,1024]{1,0:T(8,128)(2,1)}), bf16[768,8192]{1,0:T(8,128)(2,1)}) %all-gather.2.cloned.1.call-update) | async-done | bytes 12582928 | tf_op jit(solution)/shard_map/all_gather | solution.py:47
  158.5 20.0 %convolution_convert_fusion = bf16[8192,1024]{1,0:T(8,128)(2,1)} fusion(bf16[768,8192]{1,0:T(8,128)(2,1)} %all-gather.2.cloned.1.call-done, bf16[768,1024]{1,0:T(8,128)(2,1)} %fusion.3), kind=kOutput, calls=%fused_computation.3 | convolution fusion | flops 12893290496 | bytes 30932992 | tf_op jit(solution)/shard_map/dot_general | solution.py:49
  178.5 0.6 fusion.14
  179.1 10.4 %psum.15 = f32[]{:T(128)} all-reduce(f32[]{:T(128)} %fusion.14), channel_id=1, replica_groups=mesh['dp'=4,'mp'=4,'section'=2] {'dp'}, use_global_device_ids=true, to_apply=%region_8.9 | all-reduce | flops 1 | bytes 8 | tf_op jit(solution)/shard_map/psum | solution.py:56
  190.2 268.8 %reduce-scatter.2.cloned.1.call-done = bf16[2048,1024]{1,0:T(8,128)(2,1)} async-done(((bf16[8192,1024]{1,0:T(8,128)(2,1)}), bf16[2048,1024]{1,0:T(8,128)(2,1)}) %reduce-scatter.2.cloned.1.call-update) | async-done | bytes 4194320 | tf_op jit(solution)/shard_map/reduce_scatter | solution.py:48
  459.1 6.8 %convert_multiply_fusion = f32[2048,1024]{1,0:T(8,128)} fusion(bf16[2048,1024]{1,0:T(8,128)(2,1)} %reduce-scatter.2.cloned.1.call-done, f32[]{:T(128)S(6)} %div.18), kind=kLoop, calls=%fused_computation.4 | loop fusion | flops 4194304 | bytes 12582916 | tf_op jit(solution)/shard_map/mul | solution.py:57
  (21 shorter events, 0.2 us)
Async XLA Ops:
  6.5 15.6 %copy-start = (bf16[384,1024]{1,0:T(8,128)(2,1)S(1)}, bf16[384,1024]{1,0:T(8,128)(2,1)}, u32[]{:S(2)}) copy-start(bf16[384,1024]{1,0:T(8,128)(2,1)} %param.6) | copy-start | bytes 2359300
  24.9 5.6 %copy-start.2 = (bf16[1024]{0:T(1024)(128)(2,1)S(1)}, bf16[1024]{0:T(1024)(128)(2,1)}, u32[]{:S(2)}) copy-start(bf16[1024]{0:T(1024)(128)(2,1)} %param.9) | copy-start | bytes 6148
  26.2 40.0 %all-to-all-start.1 = ((bf16[4,192,1024]{2,1,0:T(8,128)(2,1)}), bf16[4,192,1024]{2,1,0:T(8,128)(2,1)S(1)}, u32[]{:S(2)}, u32[]{:S(2)}) async-start(bf16[4,192,1024]{2,1,0:T(8,128)(2,1)} %broadcast_multiply_fusion), calls=%async_computation.1 | async-start | bytes 3145728 | tf_op jit(solution)/shard_map/all_to_all | solution.py:35
  29.8 128.7 %all-gather.2.cloned.1.call-start = ((), (), s32[]{:S(2)}) async-start(), calls=%async_computation.3 | async-start | bytes 14155776 | tf_op jit(solution)/shard_map/all_gather | solution.py:47
  69.8 15.4 %copy-start.1 = (bf16[768,1024]{1,0:T(8,128)(2,1)S(1)}, bf16[768,1024]{1,0:T(8,128)(2,1)}, u32[]{:S(2)}) copy-start(bf16[768,1024]{1,0:T(8,128)(2,1)} %gather_fusion.1) | copy-start | bytes 4718596
  88.2 370.9 %reduce-scatter.2.cloned.1.call-start = ((), (), s32[]{:S(2)}) async-start(), calls=%async_computation.4 | async-start | bytes 20971520 | tf_op jit(solution)/shard_map/reduce_scatter | solution.py:48
Sparse Core Ops, SparseCore 0:
  88.3 70.1 all-gather.1
  178.7 280.3 reduce-scatter.1
where the time goes:
time: 475 us; the launch traced here: 473 us
  waiting for transfers between devices  375 us (79%)
  blocking collectives  31.8 us (7%)
  matrix products  20 us (4%)
  other arithmetic  17.4 us (4%)
  between operations  14.9 us (3%)
  local copies, waits for them, and re-layouts  10.1 us (2%)
    reduce_scatter x1, waiting for transfers between devices, body(): lax.psum_scatter(lax.dot_general(all_cols, own_cols, contract, preferred_...  269 us
    all_gather x1, waiting for transfers between devices, body(): all_cols = lax.all_gather(own_cols, ('mp', 'section'), axis=1, tiled=True)  70.3 us
    all_to_all x1, waiting for transfers between devices, body(): lax.all_to_all(outgoing, 'dp', split_axis=0, concat_axis=0, tiled=True)  35.7 us
    dot_general x1, matrix products, body(): lax.dot_general(all_cols, own_cols, contract, preferred_element_type=jnp....  20 us
    psum x1, blocking collectives, body(): squares = lax.psum(jnp.sum(widened * widened, axis=1), ('mp', 'section'))  12.6 us
    psum x1, blocking collectives, body(): live_count = lax.psum(jnp.sum(live_mask), 'dp')  10.4 us
  transfers between devices with their start and end apart: 3, of which 3 were waited for; matrix products, arithmetic and copies ran while one was open for 0% of the time, Pallas kernels for 0%

commit v1 on v0

--- a/solution.py
+++ b/solution.py
@@ -1,12 +1,21 @@
+import functools
+
 import jax
 import jax.numpy as jnp
 from jax import lax
+from jax.experimental import pallas as pl
+from jax.experimental.pallas import tpu as pltpu
 from jax.sharding import PartitionSpec as P
 
 NORM_EPS = 1e-06
-
-
-def body(text_embeds, image_rows, image_source, live_len, norm_gain):
+MESH = pl.DeviceIdType.MESH
+CHUNK = 128
+GROUP = 256
+LANES = 128
+TILE = 256
+
+
+def general_body(text_embeds, image_rows, image_source, live_len, norm_gain):
     group_count = lax.axis_size("dp")
     feature_groups = lax.axis_size(("mp", "section"))
     tok_rows = text_embeds.shape[0]
@@ -57,7 +66,314 @@
     return summed * (2.0 / live_count)
 
 
+def ring_pos(m):
+    y, x = m // 2, m % 2
+    return y * (3 - x) + (1 - y) * x
+
+
+def ring_chip(pos):
+    y = pos // 2
+    return 2 * y + (pos + y) % 2
+
+
+def loop(count, step):
+    lax.fori_loop(0, count, lambda i, carry: (step(i), carry)[1], 0)
+
+
+def hessian_kernel(
+    groups, text_ref, image_ref, code_ref, gain_ref, acc_ref, row_gain_ref,
+    cols, rows, staged, codes, facts, w_row, w_col, scaled,
+    load_sem, right_send, left_send, z_recv, ring_send, ring_recv, sib_send, sib_recv, own_sem,
+    code_send, code_recv, fact_send, fact_recv, w_send, w_recv,
+):
+    g, m, s = lax.axis_index("dp"), lax.axis_index("mp"), lax.axis_index("section")
+    images, narrow = image_ref.shape
+    tokens = cols.shape[1]
+    texts = tokens - images
+    per = tokens // CHUNK
+    members = facts.shape[0]
+    me = m * 2 + s
+    features = members * narrow
+    turn = 1 - 2 * s
+    here = ring_pos(m)
+    hop = ((here - ring_pos(g)) * turn + 4) % 4
+    next_chip = ring_chip((here + turn + 4) % 4)
+
+    def chunk(ref, b, c):
+        return ref.at[b, pl.ds(pl.multiple_of(c * CHUNK, CHUNK), CHUNK)]
+
+    def remote(src, dst, send, recv, target):
+        return pltpu.make_async_remote_copy(
+            src_ref=src, dst_ref=dst, send_sem=send, recv_sem=recv,
+            device_id=target, device_id_type=MESH,
+        )
+
+    def to_right(b, c):
+        return remote(chunk(cols, b, c), chunk(cols, b, c), right_send.at[b * per + c],
+                      z_recv.at[b * per + c], {"dp": lax.rem(g + 1, groups)})
+
+    def to_left(b, c):
+        return remote(chunk(cols, b, c), chunk(cols, b, c), left_send.at[b * per + c],
+                      z_recv.at[b * per + c], {"dp": lax.rem(g + groups - 1, groups)})
+
+    def round_ring(src, b, c):
+        return remote(chunk(src, b, c), chunk(rows.at[s], b, c), ring_send.at[b * per + c],
+                      ring_recv.at[b * per + c], {"mp": next_chip})
+
+    def to_sibling(src, b, c, half):
+        return remote(chunk(src, b, c), chunk(rows.at[half], b, c), sib_send.at[b * per + c],
+                      sib_recv.at[b * per + c], {"section": 1 - s})
+
+    def keep_own(b, c):
+        return pltpu.make_async_copy(
+            chunk(cols, b, c), chunk(rows.at[s], b, c), own_sem.at[b * per + c])
+
+    def send_code(i):
+        other = lax.rem(g + 1 + i, groups)
+        return remote(code_ref, codes.at[g], code_send.at[i], code_recv.at[g], {"dp": other})
+
+    def got_code(b):
+        return remote(code_ref, codes.at[b], code_send.at[0], code_recv.at[b], {"dp": b})
+
+    def send_w(i):
+        other = lax.rem(g + 1 + i, groups)
+        return remote(w_row.at[g], w_row.at[g], w_send.at[i], w_recv.at[g], {"dp": other})
+
+    def got_w(b):
+        return remote(w_row.at[b], w_row.at[b], w_send.at[0], w_recv.at[b], {"dp": b})
+
+    def member(i):
+        other = lax.rem(me + 1 + i, members)
+        return other, {"mp": other // 2, "section": other % 2}
+
+    def send_facts(i):
+        return remote(facts.at[me], facts.at[me], fact_send.at[i], fact_recv.at[me], member(i)[1])
+
+    def got_facts(i):
+        other, target = member(i)
+        return remote(facts.at[other], facts.at[other], fact_send.at[i], fact_recv.at[other], target)
+
+    load_image = pltpu.make_async_copy(image_ref, cols.at[g, pl.ds(0, images)], load_sem.at[0])
+    load_text = pltpu.make_async_copy(
+        text_ref.at[:, pl.ds(pl.multiple_of(s * narrow, narrow), narrow)], staged, load_sem.at[1])
+    load_image.start()
+    load_text.start()
+
+    barrier = pltpu.get_barrier_semaphore()
+
+    def greet_member(i):
+        pl.semaphore_signal(barrier, inc=1, device_id=member(i)[1], device_id_type=MESH)
+
+    def greet_group(i):
+        pl.semaphore_signal(
+            barrier, inc=1, device_id={"dp": lax.rem(g + 1 + i, groups)}, device_id_type=MESH)
+
+    loop(members - 1, greet_member)
+    loop(groups - 1, greet_group)
+    load_image.wait()
+    pl.semaphore_wait(barrier, members + groups - 2)
+
+    def send_own(c):
+        pl.when(g < groups - 1)(lambda: to_right(g, c).start())
+        pl.when(g > 0)(lambda: to_left(g, c).start())
+
+    loop(images // CHUNK, send_own)
+    loop(groups - 1, lambda i: send_code(i).start())
+
+    code = code_ref[...]
+    is_text = code < -1.5
+    before = lax.broadcasted_iota(jnp.int32, (tokens, tokens), 0)
+    after = lax.broadcasted_iota(jnp.int32, (tokens, tokens), 1)
+    upto = (before <= after).astype(jnp.float32).astype(jnp.bfloat16)
+    rank = jnp.dot(is_text.astype(jnp.float32).astype(jnp.bfloat16), upto,
+                   preferred_element_type=jnp.float32)
+    place = jnp.where(is_text, rank - 1.0, -1.0)[0:1, :]
+    slot = lax.broadcasted_iota(jnp.int32, (texts, tokens), 0).astype(jnp.float32)
+    pick = (slot == place).astype(jnp.float32).astype(jnp.bfloat16)
+    load_text.wait()
+    cols[g, pl.ds(images, texts), :] = jnp.dot(
+        pick, staged[...], preferred_element_type=jnp.float32).astype(jnp.bfloat16)
+    loop(texts // CHUNK, lambda c: send_own(c + images // CHUNK))
+
+    def is_live(values):
+        return ((values > -0.5) | ((values > -2.5) & (values < -1.5))).astype(jnp.float32)
+
+    def squares(c):
+        at = pl.multiple_of(c * LANES, LANES)
+        x = cols[g, pl.ds(at, LANES), :].astype(jnp.float32)
+        sums = jnp.sum(x * x, axis=1, keepdims=True)
+        facts[me, :, pl.ds(at, LANES)] = jnp.transpose(
+            jnp.broadcast_to(sums, (LANES, LANES)))[0:8, :]
+
+    loop(tokens // LANES, squares)
+    facts[me, :, pl.ds(tokens, narrow)] = gain_ref[...]
+    loop(members - 1, lambda i: send_facts(i).start())
+
+    row_contract = (((1,), (1,)), ((), ()))
+    live_text = lax.dot_general(is_live(code).astype(jnp.bfloat16), pick, row_contract,
+                                preferred_element_type=jnp.float32)
+    codes[g] = code
+    image_id = (lax.broadcasted_iota(jnp.int32, (images, tokens), 0) + g * images).astype(jnp.float32)
+    ones = jnp.ones((8, tokens), jnp.bfloat16)
+    live_image = jnp.zeros((8, images), jnp.float32)
+    count = jnp.zeros((8, 1), jnp.float32)
+    loop(groups - 1, lambda i: got_code(lax.rem(g + 1 + i, groups)).wait_recv())
+    for b in range(groups):
+        their = codes[b]
+        found = (image_id == their[0:1, :]).astype(jnp.float32).astype(jnp.bfloat16)
+        live_image += lax.dot_general(ones, found, row_contract, preferred_element_type=jnp.float32)
+        count += jnp.sum(is_live(their), axis=1, keepdims=True)
+    loop(members - 1, lambda i: got_facts(i).wait_recv())
+    total = facts[0, :, pl.ds(0, tokens)]
+    for d in range(1, members):
+        total += facts[d, :, pl.ds(0, tokens)]
+    factor = (2.0 / count) / (total / features + NORM_EPS)
+    w_row[g, :, pl.ds(0, images)] = factor[:, :images] * live_image
+    w_row[g, :, pl.ds(images, texts)] = factor[:, images:] * live_text
+    loop(groups - 1, lambda i: send_w(i).start())
+    for half in range(2):
+        row_gain_ref[half] = facts[2 * g + half, :, pl.ds(tokens, narrow)]
+    loop(groups - 1, lambda i: got_w(lax.rem(g + 1 + i, groups)).wait_recv())
+
+    def turn_w(b):
+        def part(c):
+            at = pl.multiple_of(c * LANES, LANES)
+            row = w_row[b, 0:1, pl.ds(at, LANES)]
+            w_col[b, pl.ds(at, LANES), :] = jnp.transpose(jnp.broadcast_to(row, (LANES, LANES)))
+        loop(tokens // LANES, part)
+
+    loop(groups, turn_w)
+
+    def clear(i):
+        acc_ref[pl.ds(pl.multiple_of(i * TILE, TILE), TILE), :] = jnp.zeros((TILE, narrow), jnp.float32)
+
+    loop(acc_ref.shape[0] // TILE, clear)
+    gain_row = gain_ref[0:1, :]
+
+    def multiply(b, at):
+        at = pl.multiple_of(at, GROUP)
+        x = cols[b, pl.ds(at, GROUP), :].astype(jnp.float32)
+        scaled[...] = (x * w_col[b, pl.ds(at, GROUP), 0:1] * gain_row).astype(jnp.bfloat16)
+        tiles = narrow // TILE
+
+        def tile(i):
+            half, lane = i // tiles, pl.multiple_of((i % tiles) * TILE, TILE)
+            out = pl.ds(pl.multiple_of(i * TILE, TILE), TILE)
+            acc_ref[out, :] += lax.dot_general(
+                rows[half, b, pl.ds(at, GROUP), pl.ds(lane, TILE)], scaled[...],
+                (((0,), (0,)), ((), ())), preferred_element_type=jnp.float32)
+
+        loop(2 * tiles, tile)
+
+    def step(t):
+        j, c = t // per, t % per
+
+        def each(side, act):
+            b = g - j + 2 * j * side
+            pl.when((b >= 0) & (b < groups) & ((j > 0) | (side == 0)))(lambda: act(b))
+
+        def pass_on(side):
+            def act(b):
+                @pl.when(j > 0)
+                def _():
+                    to_right(b, c).wait_recv()
+                    pl.when((side == 0) & (g < groups - 1))(lambda: to_right(b, c).start())
+                    pl.when((side == 1) & (g > 0))(lambda: to_left(b, c).start())
+
+            each(side, act)
+
+        def share(side):
+            def act(b):
+                @pl.when(hop == 0)
+                def _():
+                    round_ring(cols, b, c).start()
+                    to_sibling(cols, b, c, s).start()
+                    keep_own(b, c).start()
+
+                @pl.when(hop > 0)
+                def _():
+                    round_ring(cols, b, c).wait_recv()
+                    pl.when(hop < 3)(lambda: round_ring(rows.at[s], b, c).start())
+                    to_sibling(rows.at[s], b, c, s).start()
+
+            each(side, act)
+
+        def use(side):
+            def act(b):
+                to_sibling(cols, b, c, 1 - s).wait_recv()
+                pl.when(hop == 0)(lambda: keep_own(b, c).wait())
+                every = GROUP // CHUNK
+                pl.when(c % every == every - 1)(lambda: multiply(b, (c // every) * GROUP))
+
+            each(side, act)
+
+        loop(2, pass_on)
+        loop(2, share)
+        loop(2, use)
+
+    loop(groups * per, step)
+
+    def finish(i):
+        b, c = i // per, i % per
+        pl.when((b <= g) & (g < groups - 1))(lambda: to_right(b, c).wait_send())
+        pl.when((b >= g) & (g > 0))(lambda: to_left(b, c).wait_send())
+        pl.when(hop < 3)(lambda: round_ring(cols, b, c).wait_send())
+        to_sibling(cols, b, c, s).wait_send()
+
+    loop(groups * per, finish)
+    loop(groups - 1, lambda i: send_code(i).wait_send())
+    loop(groups - 1, lambda i: send_w(i).wait_send())
+    loop(members - 1, lambda i: send_facts(i).wait_send())
+
+
+def ring_body(text_embeds, image_rows, image_source, live_len, norm_gain):
+    groups = lax.axis_size("dp")
+    members = lax.axis_size(("mp", "section"))
+    tokens = text_embeds.shape[0]
+    images, narrow = image_rows.shape
+    live = jnp.arange(tokens, dtype=jnp.int32) < live_len[0]
+    code = jnp.where(image_source >= 0, jnp.where(live, image_source, -1), jnp.where(live, -2, -3))
+    code = jnp.broadcast_to(code.astype(jnp.float32)[None, :], (8, tokens))
+    gain = jnp.broadcast_to(norm_gain.astype(jnp.float32)[None, :], (8, narrow))
+    per = tokens // CHUNK
+    dma = pltpu.SemaphoreType.DMA
+    whole = pl.BlockSpec(memory_space=pltpu.VMEM)
+    far = pl.BlockSpec(memory_space=pl.ANY)
+    acc, row_gain = pl.pallas_call(
+        functools.partial(hessian_kernel, groups),
+        out_shape=(
+            jax.ShapeDtypeStruct((2 * narrow, narrow), jnp.float32),
+            jax.ShapeDtypeStruct((2, 8, narrow), jnp.float32),
+        ),
+        in_specs=[far, far, whole, whole],
+        out_specs=(whole, whole),
+        scratch_shapes=[
+            pltpu.VMEM((groups, tokens, narrow), jnp.bfloat16),
+            pltpu.VMEM((2, groups, tokens, narrow), jnp.bfloat16),
+            pltpu.VMEM((tokens, narrow), jnp.bfloat16),
+            pltpu.VMEM((groups, 8, tokens), jnp.float32),
+            pltpu.VMEM((members, 8, tokens + narrow), jnp.float32),
+            pltpu.VMEM((groups, 8, tokens), jnp.float32),
+            pltpu.VMEM((groups, tokens, LANES), jnp.float32),
+            pltpu.VMEM((GROUP, narrow), jnp.bfloat16),
+            dma((2,)),
+        ]
+        + [dma((groups * per,)) for _ in range(8)]
+        + [
+            dma((groups,)), dma((groups,)), dma((members,)), dma((members,)),
+            dma((groups,)), dma((groups,)),
+        ],
+        compiler_params=pltpu.CompilerParams(
+            collective_id=0, has_side_effects=True, vmem_limit_bytes=56 * 1024 * 1024
+        ),
+    )(text_embeds, image_rows, code, gain)
+    return acc * row_gain[:, 0, :].reshape(2 * narrow)[:, None]
+
+
 def solution(mesh):
     in_specs = (P("dp", "mp"), P("dp", ("mp", "section")), P("dp"), P("dp"), P(("mp", "section")))
     out_specs = P("dp", ("mp", "section"))
+    sizes = dict(mesh.shape)
+    ringed = sizes["dp"] == 4 and sizes["mp"] == 4 and sizes["section"] == 2
+    body = ring_body if ringed else general_body
     return jax.shard_map(body, mesh=mesh, in_specs=in_specs, out_specs=out_specs, check_vma=False)

time: 475 us -> 375 us (0.79)
  waiting for transfers between devices: 375 us -> 0 us
  Pallas kernels: 0 us -> 363 us
  blocking collectives: 31.8 us -> 0 us
  matrix products: 20 us -> 0 us
  between operations: 14.9 us -> 0.66 us
  other arithmetic: 17.4 us -> 8.08 us
  local copies, waits for them, and re-layouts: 10.1 us -> 2.75 us
    pallas_call x0 -> x1, Pallas kernels: none -> 363 us  [ring_body(): pl.pallas_call(functools.partial(hessian_kernel, groups), out_shape=(jax....]
    reduce_scatter x1 -> x0, waiting for transfers between devices: 269 us -> none  [body(): lax.psum_scatter(lax.dot_general(all_cols, own_cols, contract, preferred_...]
    all_gather x1 -> x0, waiting for transfers between devices: 70.3 us -> none  [body(): all_cols = lax.all_gather(own_cols, ('mp', 'section'), axis=1, tiled=True)]
    all_to_all x1 -> x0, waiting for transfers between devices: 35.7 us -> none  [body(): lax.all_to_all(outgoing, 'dp', split_axis=0, concat_axis=0, tiled=True)]
    psum x2 -> x0, blocking collectives: 23 us -> none  [the longest x1 12.6 us: body(): squares = lax.psum(jnp.sum(widened * widened, axis=1), ('mp', 'section'))]
    dot_general x1 -> x0, matrix products: 20 us -> none  [body(): lax.dot_general(all_cols, own_cols, contract, preferred_element_type=jnp....]
    all_to_all x1 -> x0, blocking collectives: 8.8 us -> none  [body(): lax.all_to_all(request_table.reshape(group_count, capacity), 'dp', split_...]
    gather x2 -> x0, local copies, waits for them, and re-layouts: 6.36 us -> none  [the longest x1 3.55 us: body(): picked = incoming.reshape(group_count * capacity, narrow)[wanted_slot]]
  transfers between devices with their start and end apart: 3 -> 0, of which waited for: 3 -> 0; matrix products, arithmetic and copies ran while one was open for 0% -> 0% of each run, Pallas kernels for 0% -> 0%
where the time goes in v1:
time: 375 us
  Pallas kernels  363 us (97%)
  other arithmetic  8.08 us (2%)
    pallas_call x1, Pallas kernels, ring_body(): pl.pallas_call(functools.partial(hessian_kernel, groups), out_shape=(jax....  363 us

profile of v1, /device:TPU:5, one launch (start us, length us, event | category | flops | bytes accessed | tf_op | source)
XLA Modules:
  0.0 374.8 jit_solution(16587321114991261713)
XLA Ops:
  0.7 0.7 select_convert_fusion
  1.3 0.6 broadcast_in_dim.27.code_ref
  1.9 1.3 broadcast_in_dim.28.gain_ref
  3.2 363.3 %shard_map.55 = (f32[2048,1024]{1,0:T(8,128)}, f32[2,8,1024]{2,1,0:T(8,128)}) custom-call(bf16[768,2048]{1,0:T(8,128)(2,1)} %text_ref.1, bf16[384,1024]{1,0:T(8,128)(2,1)} %image_ref.1, f32[8,768]{1,0:T(8,128)} %broadcast_in_dim.27.code_ref, f32[8,1024]{1,0:T(8,128)} %broadcast_in_dim.28.gain_ref), custom_call_target="tpu_custom_call" | custom-call | tf_op jit(solution)/shard_map/pallas_call | solution.py:342
  366.5 0.8 slice.3
  367.4 7.4 %broadcast_multiply_fusion = f32[2048,1024]{1,0:T(8,128)} fusion(f32[2048,1024]{1,0:T(8,128)} %get-tuple-element.7, f32[2048]{0:T(1024)S(1)} %bitcast.3), kind=kLoop, calls=%fused_computation | loop fusion | flops 2097152 | bytes 16785408 | tf_op jit(solution)/shard_map/mul | solution.py:370

commit v2 on v1

--- a/solution.py
+++ b/solution.py
@@ -9,9 +9,10 @@
 
 NORM_EPS = 1e-06
 MESH = pl.DeviceIdType.MESH
-CHUNK = 128
+CHUNK = 64
 GROUP = 256
 LANES = 128
+LATE = 4
 TILE = 256
 
 
@@ -81,8 +82,8 @@
 
 
 def hessian_kernel(
-    groups, text_ref, image_ref, code_ref, gain_ref, acc_ref, row_gain_ref,
-    cols, rows, staged, codes, facts, w_row, w_col, scaled,
+    groups, text_ref, image_ref, code_ref, gain_ref, out_ref, row_gain_ref,
+    acc_ref, cols, rows, staged, codes, facts, w_row, w_col, scaled,
     load_sem, right_send, left_send, z_recv, ring_send, ring_recv, sib_send, sib_recv, own_sem,
     code_send, code_recv, fact_send, fact_recv, w_send, w_recv,
 ):
@@ -159,6 +160,9 @@
     load_image.start()
     load_text.start()
 
+    def clear(i):
+        acc_ref[pl.ds(pl.multiple_of(i * TILE, TILE), TILE), :] = jnp.zeros((TILE, narrow), jnp.float32)
+
     barrier = pltpu.get_barrier_semaphore()
 
     def greet_member(i):
@@ -170,6 +174,7 @@
 
     loop(members - 1, greet_member)
     loop(groups - 1, greet_group)
+    loop(acc_ref.shape[0] // TILE, clear)
     load_image.wait()
     pl.semaphore_wait(barrier, members + groups - 2)
 
@@ -177,8 +182,8 @@
         pl.when(g < groups - 1)(lambda: to_right(g, c).start())
         pl.when(g > 0)(lambda: to_left(g, c).start())
 
+    loop(groups - 1, lambda i: send_code(i).start())
     loop(images // CHUNK, send_own)
-    loop(groups - 1, lambda i: send_code(i).start())
 
     code = code_ref[...]
     is_text = code < -1.5
@@ -233,8 +238,6 @@
     loop(groups - 1, lambda i: send_w(i).start())
     for half in range(2):
         row_gain_ref[half] = facts[2 * g + half, :, pl.ds(tokens, narrow)]
-    loop(groups - 1, lambda i: got_w(lax.rem(g + 1 + i, groups)).wait_recv())
-
     def turn_w(b):
         def part(c):
             at = pl.multiple_of(c * LANES, LANES)
@@ -242,76 +245,101 @@
             w_col[b, pl.ds(at, LANES), :] = jnp.transpose(jnp.broadcast_to(row, (LANES, LANES)))
         loop(tokens // LANES, part)
 
-    loop(groups, turn_w)
-
-    def clear(i):
-        acc_ref[pl.ds(pl.multiple_of(i * TILE, TILE), TILE), :] = jnp.zeros((TILE, narrow), jnp.float32)
-
-    loop(acc_ref.shape[0] // TILE, clear)
+    turn_w(g)
     gain_row = gain_ref[0:1, :]
-
-    def multiply(b, at):
-        at = pl.multiple_of(at, GROUP)
-        x = cols[b, pl.ds(at, GROUP), :].astype(jnp.float32)
-        scaled[...] = (x * w_col[b, pl.ds(at, GROUP), 0:1] * gain_row).astype(jnp.bfloat16)
-        tiles = narrow // TILE
-
-        def tile(i):
-            half, lane = i // tiles, pl.multiple_of((i % tiles) * TILE, TILE)
-            out = pl.ds(pl.multiple_of(i * TILE, TILE), TILE)
-            acc_ref[out, :] += lax.dot_general(
-                rows[half, b, pl.ds(at, GROUP), pl.ds(lane, TILE)], scaled[...],
-                (((0,), (0,)), ((), ())), preferred_element_type=jnp.float32)
-
-        loop(2 * tiles, tile)
+    every = GROUP // CHUNK
+    sets = tokens // GROUP
+    steps = every + (groups - 1) * per
+    tiles = narrow // TILE
+    share_tiles = 2 * tiles // every
+
+    def each(t, act):
+        @pl.when((t >= 0) & (t < every))
+        def _():
+            loop(sets, lambda e: act(e, g, e * every + t))
+
+        @pl.when((t >= every) & (t < steps))
+        def _():
+            r = t - every
+
+            def side(e):
+                b = g + (2 * e - 1) * (1 + r // per)
+                pl.when((b >= 0) & (b < groups))(lambda: act(e, b, r % per))
+
+            loop(2, side)
+
+    def pass_on(t):
+        def act(e, b, c):
+            @pl.when(t >= every)
+            def _():
+                to_right(b, c).wait_recv()
+                pl.when((e == 0) & (g < groups - 1))(lambda: to_right(b, c).start())
+                pl.when((e == 1) & (g > 0))(lambda: to_left(b, c).start())
+
+            @pl.when(hop == 0)
+            def _():
+                round_ring(cols, b, c).start()
+                to_sibling(cols, b, c, s).start()
+                keep_own(b, c).start()
+
+        each(t, act)
+
+    def take_ring(t):
+        def act(e, b, c):
+            round_ring(cols, b, c).wait_recv()
+            pl.when(hop < 3)(lambda: round_ring(rows.at[s], b, c).start())
+            to_sibling(rows.at[s], b, c, s).start()
+
+        pl.when(hop > 0)(lambda: each(t - hop, act))
+
+    def take_sibling(t):
+        def act(e, b, c):
+            to_sibling(cols, b, c, 1 - s).wait_recv()
+            pl.when(hop == 0)(lambda: keep_own(b, c).wait())
+
+        each(t, act)
+
+    def multiply(t):
+        part = t % every
+
+        def act(e, b, c):
+            at = pl.multiple_of((c // every) * GROUP, GROUP)
+
+            @pl.when((b != g) & (part == 0) & (c // every == 0))
+            def _():
+                got_w(b).wait_recv()
+                turn_w(b)
+
+            @pl.when(part == 0)
+            def _():
+                x = cols[b, pl.ds(at, GROUP), :].astype(jnp.float32)
+                scaled[e] = (x * w_col[b, pl.ds(at, GROUP), 0:1] * gain_row).astype(jnp.bfloat16)
+
+            def tile(n):
+                i = part * share_tiles + n
+                half, lane = i // tiles, pl.multiple_of((i % tiles) * TILE, TILE)
+                out = pl.ds(pl.multiple_of(i * TILE, TILE), TILE)
+                acc_ref[out, :] += lax.dot_general(
+                    rows[half, b, pl.ds(at, GROUP), pl.ds(lane, TILE)], scaled[e],
+                    (((0,), (0,)), ((), ())), preferred_element_type=jnp.float32)
+
+            loop(share_tiles, tile)
+
+        each(t, act)
 
     def step(t):
-        j, c = t // per, t % per
-
-        def each(side, act):
-            b = g - j + 2 * j * side
-            pl.when((b >= 0) & (b < groups) & ((j > 0) | (side == 0)))(lambda: act(b))
-
-        def pass_on(side):
-            def act(b):
-                @pl.when(j > 0)
-                def _():
-                    to_right(b, c).wait_recv()
-                    pl.when((side == 0) & (g < groups - 1))(lambda: to_right(b, c).start())
-                    pl.when((side == 1) & (g > 0))(lambda: to_left(b, c).start())
-
-            each(side, act)
-
-        def share(side):
-            def act(b):
-                @pl.when(hop == 0)
-                def _():
-                    round_ring(cols, b, c).start()
-                    to_sibling(cols, b, c, s).start()
-                    keep_own(b, c).start()
-
-                @pl.when(hop > 0)
-                def _():
-                    round_ring(cols, b, c).wait_recv()
-                    pl.when(hop < 3)(lambda: round_ring(rows.at[s], b, c).start())
-                    to_sibling(rows.at[s], b, c, s).start()
-
-            each(side, act)
-
-        def use(side):
-            def act(b):
-                to_sibling(cols, b, c, 1 - s).wait_recv()
-                pl.when(hop == 0)(lambda: keep_own(b, c).wait())
-                every = GROUP // CHUNK
-                pl.when(c % every == every - 1)(lambda: multiply(b, (c // every) * GROUP))
-
-            each(side, act)
-
-        loop(2, pass_on)
-        loop(2, share)
-        loop(2, use)
-
-    loop(groups * per, step)
+        pass_on(t)
+        take_ring(t)
+        take_sibling(t - LATE)
+        multiply(t - LATE - every)
+
+    loop(steps + LATE + every, step)
+
+    def write(i):
+        part = pl.ds(pl.multiple_of(i * TILE, TILE), TILE)
+        out_ref[part, :] = acc_ref[part, :].astype(out_ref.dtype)
+
+    loop(acc_ref.shape[0] // TILE, write)
 
     def finish(i):
         b, c = i // per, i % per
@@ -342,12 +370,13 @@
     acc, row_gain = pl.pallas_call(
         functools.partial(hessian_kernel, groups),
         out_shape=(
-            jax.ShapeDtypeStruct((2 * narrow, narrow), jnp.float32),
+            jax.ShapeDtypeStruct((2 * narrow, narrow), jnp.bfloat16),
             jax.ShapeDtypeStruct((2, 8, narrow), jnp.float32),
         ),
         in_specs=[far, far, whole, whole],
         out_specs=(whole, whole),
         scratch_shapes=[
+            pltpu.VMEM((2 * narrow, narrow), jnp.float32),
             pltpu.VMEM((groups, tokens, narrow), jnp.bfloat16),
             pltpu.VMEM((2, groups, tokens, narrow), jnp.bfloat16),
             pltpu.VMEM((tokens, narrow), jnp.bfloat16),
@@ -355,7 +384,7 @@
             pltpu.VMEM((members, 8, tokens + narrow), jnp.float32),
             pltpu.VMEM((groups, 8, tokens), jnp.float32),
             pltpu.VMEM((groups, tokens, LANES), jnp.float32),
-            pltpu.VMEM((GROUP, narrow), jnp.bfloat16),
+            pltpu.VMEM((tokens // GROUP, GROUP, narrow), jnp.bfloat16),
             dma((2,)),
         ]
         + [dma((groups * per,)) for _ in range(8)]
@@ -364,10 +393,10 @@
             dma((groups,)), dma((groups,)),
         ],
         compiler_params=pltpu.CompilerParams(
-            collective_id=0, has_side_effects=True, vmem_limit_bytes=56 * 1024 * 1024
+            collective_id=0, has_side_effects=True, vmem_limit_bytes=40 * 1024 * 1024
         ),
     )(text_embeds, image_rows, code, gain)
-    return acc * row_gain[:, 0, :].reshape(2 * narrow)[:, None]
+    return acc.astype(jnp.float32) * row_gain[:, 0, :].reshape(2 * narrow)[:, None]
 
 
 def solution(mesh):

time: 375 us -> 145 us (0.39)
  Pallas kernels: 363 us -> 136 us
    pallas_call x1, Pallas kernels: 363 us -> 136 us  [ring_body(): pl.pallas_call(functools.partial(hessian_kernel, groups), out_shape=(jax....]
where the time goes in v2:
time: 145 us
  Pallas kernels  136 us (94%)
  other arithmetic  4.7 us (3%)
  local copies, waits for them, and re-layouts  3.72 us (3%)
    pallas_call x1, Pallas kernels, ring_body(): pl.pallas_call(functools.partial(hessian_kernel, groups), out_shape=(jax....  136 us
    mul x1, other arithmetic, ring_body(): acc.astype(jnp.float32) * row_gain[:, 0, :].reshape(2 * narrow)[:, None]  4.01 us
    unnamed x4, local copies, waits for them, and re-layouts  3.02 us

profile of v2, /device:TPU:5, one launch (start us, length us, event | category | flops | bytes accessed | tf_op | source)
XLA Modules:
  0.0 144.7 jit_solution(13584954447545712710)
XLA Ops:
  0.7 0.7 select_convert_fusion
  1.4 0.7 broadcast_in_dim.28.gain_ref
  2.0 0.0 copy-start
  2.0 1.9 %copy-done = bf16[768,2048]{1,0:T(8,128)(2,1)S(1)} copy-done((bf16[768,2048]{1,0:T(8,128)(2,1)S(1)}, bf16[768,2048]{1,0:T(8,128)(2,1)}, u32[]{:S(2)}) %copy-start) | copy-done | bytes 3145752
  3.9 0.0 copy-start.1
  3.9 1.1 copy-done.1
  5.1 135.6 %shard_map.55 = (bf16[2048,1024]{1,0:T(8,128)(2,1)S(1)}, f32[2,8,1024]{2,1,0:T(8,128)S(1)}) custom-call(bf16[768,2048]{1,0:T(8,128)(2,1)S(1)} %copy-done, bf16[384,1024]{1,0:T(8,128)(2,1)S(1)} %copy-done.1, f32[8,768]{1,0:T(8,128)S(1)} %broadcast_in_dim.27.code_ref, f32[8,1024]{1,0:T(8,128)S(1)} %broadcast_in_dim.28.gain_ref), custom_call_target="tpu_custom_call" | custom-call | tf_op jit(solution)/shard_map/pallas_call | solution.py:370
  140.7 4.0 %convert_multiply_fusion = f32[2048,1024]{1,0:T(8,128)} fusion(bf16[2048,1024]{1,0:T(8,128)(2,1)S(1)} %get-tuple-element.7, f32[2048]{0:T(1024)S(1)} %bitcast.3), kind=kLoop, calls=%fused_computation | loop fusion | flops 4194304 | bytes 12591104 | tf_op jit(solution)/shard_map/mul | solution.py:399
  (2 shorter events, 0.0 us)
Async XLA Ops:
  2.0 1.9 %copy-start = (bf16[768,2048]{1,0:T(8,128)(2,1)S(1)}, bf16[768,2048]{1,0:T(8,128)(2,1)}, u32[]{:S(2)}) copy-start(bf16[768,2048]{1,0:T(8,128)(2,1)} %text_ref.1) | copy-start | bytes 9437188
  3.9 1.1 copy-start.1

commit v3 on v2

--- a/solution.py
+++ b/solution.py
@@ -12,7 +12,7 @@
 CHUNK = 64
 GROUP = 256
 LANES = 128
-LATE = 4
+AHEAD = 2
 TILE = 256
 
 
@@ -84,7 +84,7 @@
 def hessian_kernel(
     groups, text_ref, image_ref, code_ref, gain_ref, out_ref, row_gain_ref,
     acc_ref, cols, rows, staged, codes, facts, w_row, w_col, scaled,
-    load_sem, right_send, left_send, z_recv, ring_send, ring_recv, sib_send, sib_recv, own_sem,
+    load_sem, right_send, left_send, z_recv, ring_send, back_send, ring_recv, sib_send, sib_recv, own_sem,
     code_send, code_recv, fact_send, fact_recv, w_send, w_recv,
 ):
     g, m, s = lax.axis_index("dp"), lax.axis_index("mp"), lax.axis_index("section")
@@ -99,6 +99,10 @@
     here = ring_pos(m)
     hop = ((here - ring_pos(g)) * turn + 4) % 4
     next_chip = ring_chip((here + turn + 4) % 4)
+    back_chip = ring_chip((here - turn + 4) % 4)
+    every = GROUP // CHUNK
+    sib_lag = (4 - hop) % 4 + 1 + (3 - hop) // 3
+    lead_lag = hop - hop // 3
 
     def chunk(ref, b, c):
         return ref.at[b, pl.ds(pl.multiple_of(c * CHUNK, CHUNK), CHUNK)]
@@ -121,6 +125,13 @@
         return remote(chunk(src, b, c), chunk(rows.at[s], b, c), ring_send.at[b * per + c],
                       ring_recv.at[b * per + c], {"mp": next_chip})
 
+    def is_last(b, c):
+        return ((b - g) * (b - g) == (groups - 1) * (groups - 1)) & (c >= per - every)
+
+    def ring_back(b, c):
+        return remote(chunk(cols, b, c), chunk(rows.at[s], b, c), back_send.at[c - (per - every)],
+                      ring_recv.at[b * per + c], {"mp": back_chip})
+
     def to_sibling(src, b, c, half):
         return remote(chunk(src, b, c), chunk(rows.at[half], b, c), sib_send.at[b * per + c],
                       sib_recv.at[b * per + c], {"section": 1 - s})
@@ -131,28 +142,29 @@
 
     def send_code(i):
         other = lax.rem(g + 1 + i, groups)
-        return remote(code_ref, codes.at[g], code_send.at[i], code_recv.at[g], {"dp": other})
+        return remote(code_ref.at[pl.ds(0, 1)], codes.at[g, pl.ds(0, 1)], code_send.at[i], code_recv.at[g], {"dp": other})
 
     def got_code(b):
-        return remote(code_ref, codes.at[b], code_send.at[0], code_recv.at[b], {"dp": b})
+        return remote(code_ref.at[pl.ds(0, 1)], codes.at[b, pl.ds(0, 1)], code_send.at[0], code_recv.at[b], {"dp": b})
 
     def send_w(i):
         other = lax.rem(g + 1 + i, groups)
-        return remote(w_row.at[g], w_row.at[g], w_send.at[i], w_recv.at[g], {"dp": other})
+        return remote(w_row.at[g, pl.ds(0, 1)], w_row.at[g, pl.ds(0, 1)], w_send.at[i], w_recv.at[g], {"dp": other})
 
     def got_w(b):
-        return remote(w_row.at[b], w_row.at[b], w_send.at[0], w_recv.at[b], {"dp": b})
+        return remote(w_row.at[b, pl.ds(0, 1)], w_row.at[b, pl.ds(0, 1)], w_send.at[0], w_recv.at[b], {"dp": b})
 
     def member(i):
         other = lax.rem(me + 1 + i, members)
         return other, {"mp": other // 2, "section": other % 2}
 
     def send_facts(i):
-        return remote(facts.at[me], facts.at[me], fact_send.at[i], fact_recv.at[me], member(i)[1])
+        return remote(facts.at[me, pl.ds(0, 1)], facts.at[me, pl.ds(0, 1)], fact_send.at[i], fact_recv.at[me], member(i)[1])
 
     def got_facts(i):
         other, target = member(i)
-        return remote(facts.at[other], facts.at[other], fact_send.at[i], fact_recv.at[other], target)
+        return remote(facts.at[other, pl.ds(0, 1)], facts.at[other, pl.ds(0, 1)], fact_send.at[i],
+                      fact_recv.at[other], target)
 
     load_image = pltpu.make_async_copy(image_ref, cols.at[g, pl.ds(0, images)], load_sem.at[0])
     load_text = pltpu.make_async_copy(
@@ -198,7 +210,7 @@
     load_text.wait()
     cols[g, pl.ds(images, texts), :] = jnp.dot(
         pick, staged[...], preferred_element_type=jnp.float32).astype(jnp.bfloat16)
-    loop(texts // CHUNK, lambda c: send_own(c + images // CHUNK))
+    loop(AHEAD, lambda c: send_own(c + images // CHUNK))
 
     def is_live(values):
         return ((values > -0.5) | ((values > -2.5) & (values < -1.5))).astype(jnp.float32)
@@ -207,37 +219,39 @@
         at = pl.multiple_of(c * LANES, LANES)
         x = cols[g, pl.ds(at, LANES), :].astype(jnp.float32)
         sums = jnp.sum(x * x, axis=1, keepdims=True)
-        facts[me, :, pl.ds(at, LANES)] = jnp.transpose(
-            jnp.broadcast_to(sums, (LANES, LANES)))[0:8, :]
+        facts[me, 0:1, pl.ds(at, LANES)] = jnp.transpose(
+            jnp.broadcast_to(sums, (LANES, LANES)))[0:1, :]
 
     loop(tokens // LANES, squares)
-    facts[me, :, pl.ds(tokens, narrow)] = gain_ref[...]
+    facts[me, 0:1, pl.ds(tokens, narrow)] = gain_ref[0:1, :]
     loop(members - 1, lambda i: send_facts(i).start())
 
     row_contract = (((1,), (1,)), ((), ()))
     live_text = lax.dot_general(is_live(code).astype(jnp.bfloat16), pick, row_contract,
                                 preferred_element_type=jnp.float32)
-    codes[g] = code
+    codes[g, 0:1, :] = code[0:1, :]
     image_id = (lax.broadcasted_iota(jnp.int32, (images, tokens), 0) + g * images).astype(jnp.float32)
     ones = jnp.ones((8, tokens), jnp.bfloat16)
     live_image = jnp.zeros((8, images), jnp.float32)
-    count = jnp.zeros((8, 1), jnp.float32)
+    count = jnp.zeros((1, 1), jnp.float32)
     loop(groups - 1, lambda i: got_code(lax.rem(g + 1 + i, groups)).wait_recv())
     for b in range(groups):
-        their = codes[b]
-        found = (image_id == their[0:1, :]).astype(jnp.float32).astype(jnp.bfloat16)
+        their = codes[b, 0:1, :]
+        found = (image_id == their).astype(jnp.float32).astype(jnp.bfloat16)
         live_image += lax.dot_general(ones, found, row_contract, preferred_element_type=jnp.float32)
         count += jnp.sum(is_live(their), axis=1, keepdims=True)
     loop(members - 1, lambda i: got_facts(i).wait_recv())
-    total = facts[0, :, pl.ds(0, tokens)]
+    total = facts[0, 0:1, pl.ds(0, tokens)]
     for d in range(1, members):
-        total += facts[d, :, pl.ds(0, tokens)]
+        total += facts[d, 0:1, pl.ds(0, tokens)]
     factor = (2.0 / count) / (total / features + NORM_EPS)
-    w_row[g, :, pl.ds(0, images)] = factor[:, :images] * live_image
-    w_row[g, :, pl.ds(images, texts)] = factor[:, images:] * live_text
+    w_row[g, 0:1, pl.ds(0, images)] = factor[:, :images] * live_image[0:1, :]
+    w_row[g, 0:1, pl.ds(images, texts)] = factor[:, images:] * live_text[0:1, :]
     loop(groups - 1, lambda i: send_w(i).start())
+    loop(texts // CHUNK - AHEAD, lambda c: send_own(c + images // CHUNK + AHEAD))
     for half in range(2):
-        row_gain_ref[half] = facts[2 * g + half, :, pl.ds(tokens, narrow)]
+        row_gain_ref[half] = jnp.broadcast_to(
+            facts[2 * g + half, 0:1, pl.ds(tokens, narrow)], (8, narrow))
     def turn_w(b):
         def part(c):
             at = pl.multiple_of(c * LANES, LANES)
@@ -247,11 +261,10 @@
 
     turn_w(g)
     gain_row = gain_ref[0:1, :]
-    every = GROUP // CHUNK
     sets = tokens // GROUP
     steps = every + (groups - 1) * per
     tiles = narrow // TILE
-    share_tiles = 2 * tiles // every
+    share_tiles = tiles // every
 
     def each(t, act):
         @pl.when((t >= 0) & (t < every))
@@ -279,6 +292,7 @@
             @pl.when(hop == 0)
             def _():
                 round_ring(cols, b, c).start()
+                pl.when(is_last(b, c))(lambda: ring_back(b, c).start())
                 to_sibling(cols, b, c, s).start()
                 keep_own(b, c).start()
 
@@ -287,7 +301,8 @@
     def take_ring(t):
         def act(e, b, c):
             round_ring(cols, b, c).wait_recv()
-            pl.when(hop < 3)(lambda: round_ring(rows.at[s], b, c).start())
+            pl.when((hop == 1) | ((hop == 2) & ~is_last(b, c)))(
+                lambda: round_ring(rows.at[s], b, c).start())
             to_sibling(rows.at[s], b, c, s).start()
 
         pl.when(hop > 0)(lambda: each(t - hop, act))
@@ -295,33 +310,40 @@
     def take_sibling(t):
         def act(e, b, c):
             to_sibling(cols, b, c, 1 - s).wait_recv()
-            pl.when(hop == 0)(lambda: keep_own(b, c).wait())
 
         each(t, act)
 
-    def multiply(t):
-        part = t % every
-
+    def weigh(t):
         def act(e, b, c):
             at = pl.multiple_of((c // every) * GROUP, GROUP)
 
-            @pl.when((b != g) & (part == 0) & (c // every == 0))
+            @pl.when((b != g) & (c == 0))
             def _():
                 got_w(b).wait_recv()
                 turn_w(b)
 
-            @pl.when(part == 0)
-            def _():
-                x = cols[b, pl.ds(at, GROUP), :].astype(jnp.float32)
-                scaled[e] = (x * w_col[b, pl.ds(at, GROUP), 0:1] * gain_row).astype(jnp.bfloat16)
+            x = cols[b, pl.ds(at, GROUP), :].astype(jnp.float32)
+            scaled[(t // every) % 2 * sets + e] = (
+                x * w_col[b, pl.ds(at, GROUP), 0:1] * gain_row).astype(jnp.bfloat16)
+
+        pl.when((t >= 0) & (t % every == 0))(lambda: each(t, act))
+
+    def multiply(t, half):
+        def act(e, b, c):
+            at = pl.multiple_of((c // every) * GROUP, GROUP)
 
             def tile(n):
-                i = part * share_tiles + n
-                half, lane = i // tiles, pl.multiple_of((i % tiles) * TILE, TILE)
-                out = pl.ds(pl.multiple_of(i * TILE, TILE), TILE)
-                acc_ref[out, :] += lax.dot_general(
-                    rows[half, b, pl.ds(at, GROUP), pl.ds(lane, TILE)], scaled[e],
+                i = (t % every) * share_tiles + n
+                out = pl.ds(pl.multiple_of(half * narrow + i * TILE, TILE), TILE)
+                value = acc_ref[out, :] + lax.dot_general(
+                    rows[half, b, pl.ds(at, GROUP), pl.ds(pl.multiple_of(i * TILE, TILE), TILE)],
+                    scaled[(t // every) % 2 * sets + e],
                     (((0,), (0,)), ((), ())), preferred_element_type=jnp.float32)
+                acc_ref[out, :] = value
+
+                @pl.when(t >= steps - every)
+                def _():
+                    out_ref[out, :] = value.astype(out_ref.dtype)
 
             loop(share_tiles, tile)
 
@@ -330,22 +352,29 @@
     def step(t):
         pass_on(t)
         take_ring(t)
-        take_sibling(t - LATE)
-        multiply(t - LATE - every)
-
-    loop(steps + LATE + every, step)
-
-    def write(i):
-        part = pl.ds(pl.multiple_of(i * TILE, TILE), TILE)
-        out_ref[part, :] = acc_ref[part, :].astype(out_ref.dtype)
-
-    loop(acc_ref.shape[0] // TILE, write)
+        pl.when(hop == 0)(lambda: each(t - 1, lambda e, b, c: keep_own(b, c).wait()))
+        take_sibling(t - sib_lag)
+        weigh(t - lead_lag - every)
+        multiply(t - hop - every, s)
+        multiply(t - sib_lag - every, 1 - s)
+
+    loop(steps + 4 + every, step)
+
+    @pl.when((g > 0) & (g < groups - 1))
+    def _():
+        def write(i):
+            part = pl.ds(pl.multiple_of(i * TILE, TILE), TILE)
+            out_ref[part, :] = acc_ref[part, :].astype(out_ref.dtype)
+
+        loop(acc_ref.shape[0] // TILE, write)
 
     def finish(i):
         b, c = i // per, i % per
         pl.when((b <= g) & (g < groups - 1))(lambda: to_right(b, c).wait_send())
         pl.when((b >= g) & (g > 0))(lambda: to_left(b, c).wait_send())
-        pl.when(hop < 3)(lambda: round_ring(cols, b, c).wait_send())
+        pl.when((hop < 2) | ((hop == 2) & ~is_last(b, c)))(
+            lambda: round_ring(cols, b, c).wait_send())
+        pl.when((hop == 0) & is_last(b, c))(lambda: ring_back(b, c).wait_send())
         to_sibling(cols, b, c, s).wait_send()
 
     loop(groups * per, finish)
@@ -384,10 +413,12 @@
             pltpu.VMEM((members, 8, tokens + narrow), jnp.float32),
             pltpu.VMEM((groups, 8, tokens), jnp.float32),
             pltpu.VMEM((groups, tokens, LANES), jnp.float32),
-            pltpu.VMEM((tokens // GROUP, GROUP, narrow), jnp.bfloat16),
+            pltpu.VMEM((2 * (tokens // GROUP), GROUP, narrow), jnp.bfloat16),
             dma((2,)),
         ]
-        + [dma((groups * per,)) for _ in range(8)]
+        + [dma((groups * per,)) for _ in range(4)]
+        + [dma((GROUP // CHUNK,))]
+        + [dma((groups * per,)) for _ in range(4)]
         + [
             dma((groups,)), dma((groups,)), dma((members,)), dma((members,)),
             dma((groups,)), dma((groups,)),

time: 145 us -> 140 us (0.966)
  the two profiles are of different devices: /device:TPU:5 before, /device:TPU:7 now
where the time goes in v3:
time: 140 us; the launch traced here: 139 us
  Pallas kernels  130 us (93%)
  other arithmetic  4.7 us (3%)
  local copies, waits for them, and re-layouts  3.72 us (3%)
    pallas_call x1, Pallas kernels, ring_body(): pl.pallas_call(functools.partial(hessian_kernel, groups), out_shape=(jax....  130 us
    mul x1, other arithmetic, ring_body(): acc.astype(jnp.float32) * row_gain[:, 0, :].reshape(2 * narrow)[:, None]  4.01 us
    unnamed x4, local copies, waits for them, and re-layouts  3.02 us

profile of v3, /device:TPU:7, one launch (start us, length us, event | category | flops | bytes accessed | tf_op | source)
XLA Modules:
  0.0 139.4 jit_solution(3271358278842816651)
XLA Ops:
  0.7 0.7 select_convert_fusion
  1.4 0.7 broadcast_in_dim.28.gain_ref
  2.0 0.0 copy-start
  2.0 1.9 %copy-done = bf16[768,2048]{1,0:T(8,128)(2,1)S(1)} copy-done((bf16[768,2048]{1,0:T(8,128)(2,1)S(1)}, bf16[768,2048]{1,0:T(8,128)(2,1)}, u32[]{:S(2)}) %copy-start) | copy-done | bytes 3145752
  3.9 0.0 copy-start.1
  3.9 1.1 copy-done.1
  5.1 130.3 %shard_map.55 = (bf16[2048,1024]{1,0:T(8,128)(2,1)S(1)}, f32[2,8,1024]{2,1,0:T(8,128)S(1)}) custom-call(bf16[768,2048]{1,0:T(8,128)(2,1)S(1)} %copy-done, bf16[384,1024]{1,0:T(8,128)(2,1)S(1)} %copy-done.1, f32[8,768]{1,0:T(8,128)S(1)} %broadcast_in_dim.27.code_ref, f32[8,1024]{1,0:T(8,128)S(1)} %broadcast_in_dim.28.gain_ref), custom_call_target="tpu_custom_call" | custom-call | tf_op jit(solution)/shard_map/pallas_call | solution.py:399
  135.4 4.0 %convert_multiply_fusion = f32[2048,1024]{1,0:T(8,128)} fusion(bf16[2048,1024]{1,0:T(8,128)(2,1)S(1)} %get-tuple-element.7, f32[2048]{0:T(1024)S(1)} %bitcast.3), kind=kLoop, calls=%fused_computation | loop fusion | flops 4194304 | bytes 12591104 | tf_op jit(solution)/shard_map/mul | solution.py:430
  (2 shorter events, 0.0 us)
Async XLA Ops:
  2.0 1.9 %copy-start = (bf16[768,2048]{1,0:T(8,128)(2,1)S(1)}, bf16[768,2048]{1,0:T(8,128)(2,1)}, u32[]{:S(2)}) copy-start(bf16[768,2048]{1,0:T(8,128)(2,1)} %text_ref.1) | copy-start | bytes 9437188
  3.9 1.1 copy-start.1
